TPU v7x, 512 devices: a whole 4x8x8 slice. The times are simulated.
512 devices in a mesh: row: 16 (over z, core), col: 32 (over x, y).
Axes of the slice: x: 4, y: 8, z: 8, core: 2. Of those that a mesh axis runs over, the one named last changes fastest.
Arguments:
- slip_load: bfloat16 [16, 32, 1024, 128], P('row', 'col'), may hold values from -6 to 6
- flexibility: bfloat16 [16, 32, 1024, 1024], P('row', 'col'), as said below
- schur: bfloat16 [16, 32, 1024, 1024], P('row', 'col'), as said below
- corner_coupling: float32 [16, 32, 12, 1024], P('row', 'col'), may hold values from -0.1875 to 0.1875
- coarse_inverse: float32 [6144, 6144], P('row', 'col'), as said below
- bounds_table: float32 [16], replicated, may hold values from 0.3 to 3
- bound_index: int32 [16, 32, 1024], P('row', 'col'), may hold values from 0 to 15
- face_rows: int32 [16, 32, 4], P('row', 'col'), may hold values from 0 to 256, as said below
Outputs:
- multipliers: bfloat16 [16, 32, 1024, 128], P('row', 'col')
Inputs may be any that keep to these rules, and one draw needn't show every extreme that they name: `face_rows`: face counts agree between the two subdomains of a shared face, are 0 on faces at the edge of the grid, and some face has exactly 256 live slots. `coarse_inverse`: symmetric. `flexibility`: symmetric and positive definite. `schur`: symmetric and positive definite.
All inputs are finite; a program needn't handle non-finite values.
Results may differ from a plain program's by a relative error of at most 0.0038.
Values sent between devices are 32-bit elements; how exact they have to be, the bound alone decides.
A program may use at most 64 MiB of HBM per device.

v0:
```python
import jax
import jax.numpy as jnp
from jax import lax
from jax.sharding import Mesh
from jax.sharding import PartitionSpec as P

ITERS = 2
ROW = ("row_0", "row_1")
COL = ("col_0", "col_1")


def passed_along(x, axis, by):
    count = lax.axis_size(axis)
    pairs = [(i, i + by) for i in range(count) if 0 <= i + by < count]
    return lax.ppermute(x, axis, pairs)


def joined_along(tiles, dim):
    shape = list(tiles.shape[1:])
    shape[dim] *= tiles.shape[0]
    return jnp.moveaxis(tiles, 0, dim).reshape(shape)


def from_everyone(x, axis):
    copies = jnp.broadcast_to(x, (lax.axis_size(axis), *x.shape))
    return lax.all_to_all(copies, axis, split_axis=0, concat_axis=0, tiled=True)


def gather_directly(x, axis, dim):
    return joined_along(from_everyone(x, axis), dim)


def split_up(x, dim, count):
    shape = x.shape
    tiles = x.reshape(*shape[:dim], count, shape[dim] // count, *shape[dim + 1 :])
    return jnp.moveaxis(tiles, dim, 0)


def sent_and_summed(x, axis, dim):
    tiles = split_up(x, dim, lax.axis_size(axis))
    arrived = lax.all_to_all(tiles, axis, split_axis=0, concat_axis=0, tiled=True)
    return arrived.sum(axis=0)


def rows_for(lines, count):
    spare = -lines.shape[0] % count
    if not spare:
        return lines
    return jnp.concatenate([lines, jnp.zeros((spare, *lines.shape[1:]), lines.dtype)])


def nested_sum(x, axes):
    lines = x.reshape(-1, x.shape[-1])
    own = sent_and_summed(rows_for(lines, lax.axis_size(axes)), axes, 0)
    whole = gather_directly(own, axes, 0)
    return whole[: len(lines)].reshape(x.shape)


def picked_2(x, axis, root):
    return lax.dynamic_index_in_dim(lax.all_gather(x, axis), root, 0, keepdims=False)


def taken_together(x, axis):
    everything = from_everyone(x, axis)
    return jnp.sum(everything, axis=0)


def by_axis(x, axes):
    far, near = axes
    return taken_together(taken_together(x, near), far)


def packed_total(arrays, axis):
    ends = [0]
    for a in arrays:
        ends.append(ends[-1] + a.size)
    total = by_axis(jnp.concatenate([a.ravel() for a in arrays]), axis)
    return tuple((total[b:e].reshape(a.shape) for a, b, e in zip(arrays, ends, ends[1:])))


def local(
    slip_load,
    flexibility,
    schur,
    corner_coupling,
    coarse_inverse,
    bounds_table,
    bound_index,
    face_rows,
):
    loads = slip_load[0, 0].astype(jnp.float32)
    flex_block = flexibility[0, 0]
    schur_block = schur[0, 0]
    coupling = corner_coupling[0, 0]
    row_count = flex_block.shape[0]
    face_size = row_count // 4
    corners = coupling.shape[0]
    row_devices = lax.axis_size(ROW)
    row_index = lax.axis_index(ROW)
    col_index = lax.axis_index(COL)
    levels = jnp.arange(bounds_table.shape[0], dtype=jnp.int32)
    onehot = (bound_index[0, 0][:, None] == levels[None, :]).astype(jnp.float32)
    bound = jnp.sum(onehot * bounds_table[None, :], axis=1)[:, None]
    slots = jnp.arange(face_size, dtype=jnp.int32)
    live = (slots[None, :] < face_rows[0, 0][:, None]).astype(jnp.float32).reshape(row_count, 1)
    lam = jnp.clip(loads, -bound, bound)
    for iteration in range(ITERS):
        displacement = jnp.dot(
            flex_block, lam.astype(jnp.bfloat16), preferred_element_type=jnp.float32
        )
        nb_west = passed_along(displacement[face_size : 2 * face_size], COL, 1)
        nb_east = passed_along(displacement[0:face_size], COL, -1)
        nb_lower = passed_along(displacement[3 * face_size :], ROW, 1)
        nb_upper = passed_along(displacement[2 * face_size : 3 * face_size], ROW, -1)
        paired = jnp.concatenate([nb_west, nb_east, nb_lower, nb_upper], axis=0)
        jump = live * (displacement - paired - loads)
        corner_force = jnp.dot(coupling, jump, precision=lax.Precision.HIGHEST)
        gathered = gather_directly(corner_force, ROW, 0)
        partial_value = jnp.dot(coarse_inverse, gathered, precision=lax.Precision.HIGHEST)
        total = nested_sum(partial_value, COL)
        picked = picked_2(total, ROW, col_index // 2)
        offset = col_index % 2 * (corners * row_devices) + row_index * corners
        coarse = lax.dynamic_slice_in_dim(picked, offset, corners, 0)
        correction = lax.dot_general(
            coupling, coarse, (((0,), (0,)), ((), ())), precision=lax.Precision.HIGHEST
        )
        projected = jump - correction
        projected_b = projected.astype(jnp.bfloat16)
        search = jnp.dot(schur_block, projected_b, preferred_element_type=jnp.float32)
        gain_local = jnp.sum(projected_b.astype(jnp.float32) * search, axis=0)
        search_b = search.astype(jnp.bfloat16)
        curved = jnp.dot(flex_block, search_b, preferred_element_type=jnp.float32)
        curve_local = jnp.sum(search_b.astype(jnp.float32) * curved, axis=0)
        gain, curvature = packed_total(
            (gain_local, curve_local), (("row_0", "row_1"), ("col_0", "col_1"))
        )
        lam = jnp.clip(lam - (gain / curvature)[None, :] * search, -bound, bound)
    return lam.astype(jnp.bfloat16)[None, None]


def solution(mesh):
    finer = Mesh(mesh.devices.reshape(8, 2, 4, 8), ("row_0", "row_1", "col_0", "col_1"))
    placed = (
        P(ROW, COL, None, None),
        P(ROW, COL, None, None),
        P(ROW, COL, None, None),
        P(ROW, COL, None, None),
        P(ROW, COL),
        P(),
        P(ROW, COL, None),
        P(ROW, COL, None),
    )
    return jax.shard_map(
        local, mesh=finer, in_specs=placed, out_specs=P(ROW, COL, None, None), check_vma=False
    )
```

profile of v0, /device:TPU:1, one launch (start us, length us, event | category | flops | bytes accessed | tf_op | source)
XLA Modules:
  0.0 317.5 jit_solution(1276120080388736159)
XLA Ops:
  6.5 0.9 select_reduce_fusion
  7.5 1.1 copy.23
  8.6 0.0 copy-start.16
  8.6 0.0 copy-start.4
  8.6 2.4 fusion.14
  11.0 0.0 copy-start.3
  11.1 4.2 %collective-permute-start = (f32[256,128]{0,1:T(8,128)S(1)}, f32[256,128]{0,1:T(8,128)S(1)}, u32[]{:S(2)}, u32[]{:S(2)}) collective-permute-start(f32[256,128]{0,1:T(8,128)S(1)} %get-tuple-element.9), channel_id=1, source_target_pairs={{0,1},{1,2},{2,3},{3,4},{4,5},{5,6},{6,7},{7,8},{8,9},{9,10},{10,1... | collective-permute-start | bytes 393224 | tf_op jit(solution)/shard_map/ppermute | solution.py:15
  15.3 6.0 %collective-permute-start.3 = (f32[256,128]{0,1:T(8,128)S(1)}, f32[256,128]{0,1:T(8,128)S(1)}, u32[]{:S(2)}, u32[]{:S(2)}) collective-permute-start(f32[256,128]{0,1:T(8,128)S(1)} %get-tuple-element.10), channel_id=1, source_target_pairs={{32,0},{64,32},{96,64},{128,96},{160,128},{192,160},{224,192},{256... | collective-permute-start | bytes 393224 | tf_op jit(solution)/shard_map/ppermute | solution.py:15
  21.3 1.9 collective-permute-start.2
  23.3 1.3 collective-permute-start.1
  24.6 0.1 convert_bitcast_fusion.1
  24.7 0.0 collective-permute-done
  24.7 0.0 collective-permute-done.3
  24.7 0.5 collective-permute-done.2
  25.2 4.5 %collective-permute-done.1 = f32[256,128]{0,1:T(8,128)S(1)} collective-permute-done((f32[256,128]{0,1:T(8,128)S(1)}, f32[256,128]{0,1:T(8,128)S(1)}, u32[]{:S(2)}, u32[]{:S(2)}) %collective-permute-start.1) | collective-permute-done | bytes 131104 | tf_op jit(solution)/shard_map/ppermute | solution.py:15
  29.7 0.6 convolution_bitcast_fusion.5
  30.3 0.0 copy-done.7
  30.3 0.0 copy-done.11
  30.4 18.3 %all_to_all.54 = f32[16,12,128]{2,1,0:T(8,128)S(1)} all-to-all(f32[16,12,128]{2,1,0:T(8,128)S(1)} %broadcast_in_dim.33), channel_id=1, replica_groups=mesh['row_0'=8,'row_1'=2,'col_0'=4,'col_1'=8] {'row_0','row_1'}, dimensions={0} | all-to-all | bytes 196608 | tf_op jit(solution)/shard_map/all_to_all | solution.py:26
  48.6 0.6 reshape.72
  49.3 1.3 convolution_bitcast_fusion.3
  50.6 0.1 copy.24
  50.8 20.5 %all_to_all.55 = f32[32,12,128]{2,1,0:T(8,128)S(1)} all-to-all(f32[32,12,128]{2,1,0:T(8,128)S(1)} %reshape.73), channel_id=1, replica_groups=mesh['row_0'=8,'row_1'=2,'col_0'=4,'col_1'=8] {'col_0','col_1'}, dimensions={0} | all-to-all | bytes 393216 | tf_op jit(solution)/shard_map/all_to_all | solution.py:41
  71.3 15.7 %all_to_all.56 = f32[32,12,128]{2,1,0:T(8,128)S(1)} all-to-all(f32[32,12,128]{2,1,0:T(8,128)S(1)} %broadcast_in_dim.34), channel_id=1, replica_groups=mesh['row_0'=8,'row_1'=2,'col_0'=4,'col_1'=8] {'col_0','col_1'}, dimensions={0} | all-to-all | bytes 393216 | tf_op jit(solution)/shard_map/all_to_all | solution.py:26
  87.0 0.7 all_gather_reshape.6
  87.7 0.0 all-gather.3.cloned.1.call-update
  87.7 0.0 all-gather.5.cloned.1.call-start
  87.8 38.7 %all-gather.3.cloned.1.call-done = f32[16,384,128]{2,1,0:T(8,128)} async-done(((f32[1,384,128]{2,1,0:T(8,128)}), f32[16,384,128]{2,1,0:T(8,128)}) %all-gather.3.cloned.1.call-update) | async-done | bytes 3145744 | tf_op jit(solution)/shard_map/all_gather | solution.py:60
  126.5 1.9 fusion.39
  128.4 0.9 multiply_reduce_fusion.1
  129.3 0.9 fusion.40
  130.2 17.9 %all_to_all.57 = f32[32,1,256]{2,1,0:T(1,128)S(1)} all-to-all(f32[32,1,256]{2,1,0:T(1,128)S(1)} %broadcast_in_dim.35), channel_id=1, replica_groups=mesh['row_0'=8,'row_1'=2,'col_0'=4,'col_1'=8] {'col_0','col_1'}, dimensions={0} | all-to-all | bytes 65536 | tf_op jit(solution)/shard_map/all_to_all | solution.py:26
  148.1 0.1 reduce_sum.103
  148.2 12.9 %all_to_all.58 = f32[16,1,256]{2,1,0:T(1,128)S(1)} all-to-all(f32[16,1,256]{2,1,0:T(1,128)S(1)} %broadcast_in_dim.36), channel_id=1, replica_groups=mesh['row_0'=8,'row_1'=2,'col_0'=4,'col_1'=8] {'row_0','row_1'}, dimensions={0} | all-to-all | bytes 32768 | tf_op jit(solution)/shard_map/all_to_all | solution.py:26
  161.2 2.4 fusion.20
  163.7 2.4 collective-permute-start.4
  166.0 2.6 collective-permute-start.7
  168.6 3.0 collective-permute-start.6
  171.6 1.3 collective-permute-start.5
  172.9 0.0 collective-permute-done.4
  172.9 0.0 collective-permute-done.7
  173.0 0.6 collective-permute-done.6
  173.6 5.3 %collective-permute-done.5 = f32[256,128]{0,1:T(8,128)S(1)} collective-permute-done((f32[256,128]{0,1:T(8,128)S(1)}, f32[256,128]{0,1:T(8,128)S(1)}, u32[]{:S(2)}, u32[]{:S(2)}) %collective-permute-start.5) | collective-permute-done | bytes 131104 | tf_op jit(solution)/shard_map/ppermute | solution.py:15
  178.8 0.6 convolution_bitcast_fusion.4
  179.5 0.0 copy-done.15
  179.5 12.0 %all_to_all.59 = f32[16,12,128]{2,1,0:T(8,128)S(1)} all-to-all(f32[16,12,128]{2,1,0:T(8,128)S(1)} %broadcast_in_dim.37), channel_id=1, replica_groups=mesh['row_0'=8,'row_1'=2,'col_0'=4,'col_1'=8] {'row_0','row_1'}, dimensions={0} | all-to-all | bytes 196608 | tf_op jit(solution)/shard_map/all_to_all | solution.py:26
  191.5 0.6 reshape.74
  192.1 2.1 convolution_bitcast_fusion.2
  194.3 1.7 copy.27
  196.0 1.6 reshape.75
  197.6 18.3 %all_to_all.60 = f32[32,12,128]{2,1,0:T(8,128)} all-to-all(f32[32,12,128]{2,1,0:T(8,128)} %reshape.75), channel_id=1, replica_groups=mesh['row_0'=8,'row_1'=2,'col_0'=4,'col_1'=8] {'col_0','col_1'}, dimensions={0} | all-to-all | bytes 393216 | tf_op jit(solution)/shard_map/all_to_all | solution.py:41
  216.0 1.0 reduce_sum.105
  217.0 15.7 %all_to_all.61 = f32[32,12,128]{2,1,0:T(8,128)} all-to-all(f32[32,12,128]{2,1,0:T(8,128)S(1)} %broadcast_in_dim.38), channel_id=1, replica_groups=mesh['row_0'=8,'row_1'=2,'col_0'=4,'col_1'=8] {'col_0','col_1'}, dimensions={0} | all-to-all | bytes 393216 | tf_op jit(solution)/shard_map/all_to_all | solution.py:26
  232.7 1.6 all_gather_reshape.7
  234.4 0.0 all-gather.5.cloned.1.call-update
  234.4 38.7 %all-gather.5.cloned.1.call-done = f32[16,384,128]{2,1,0:T(8,128)} async-done(((f32[1,384,128]{2,1,0:T(8,128)}), f32[16,384,128]{2,1,0:T(8,128)}) %all-gather.5.cloned.1.call-update) | async-done | bytes 3145744 | tf_op jit(solution)/shard_map/all_gather | solution.py:60
  273.1 1.9 fusion.38
  275.0 0.9 multiply_reduce_fusion
  276.0 0.9 fusion.43
  276.9 17.9 %all_to_all.62 = f32[32,1,256]{2,1,0:T(1,128)S(1)} all-to-all(f32[32,1,256]{2,1,0:T(1,128)S(1)} %broadcast_in_dim.39), channel_id=1, replica_groups=mesh['row_0'=8,'row_1'=2,'col_0'=4,'col_1'=8] {'col_0','col_1'}, dimensions={0} | all-to-all | bytes 65536 | tf_op jit(solution)/shard_map/all_to_all | solution.py:26
  294.8 0.1 reduce_sum.108
  294.9 12.9 %all_to_all.63 = f32[16,1,256]{2,1,0:T(1,128)S(1)} all-to-all(f32[16,1,256]{2,1,0:T(1,128)S(1)} %broadcast_in_dim.40), channel_id=1, replica_groups=mesh['row_0'=8,'row_1'=2,'col_0'=4,'col_1'=8] {'row_0','row_1'}, dimensions={0} | all-to-all | bytes 32768 | tf_op jit(solution)/shard_map/all_to_all | solution.py:26
  307.8 1.0 fusion.57
  308.8 1.8 copy.30
  (49 shorter events, 0.5 us)
Async XLA Ops:
  6.5 121.8 %copy-start = (bf16[1,1,1024,1024]{3,2,1,0:T(8,128)(2,1)S(1)}, bf16[1,1,1024,1024]{3,2,1,0:T(8,128)(2,1)}, u32[]{:S(2)}) copy-start(bf16[1,1,1024,1024]{3,2,1,0:T(8,128)(2,1)} %param.10) | copy-start | bytes 6291460
  6.5 119.9 %all-gather.3.cloned.1.call-start = ((), (), s32[]{:S(2)}) async-start(), calls=%async_computation.10 | async-start | bytes 3342336 | tf_op jit(solution)/shard_map/all_gather | solution.py:60
  8.6 16.0 %copy-start.16 = (s32[1,1,4]{2,1,0:T(1,128)S(1)}, s32[1,1,4]{2,1,0:T(1,128)}, u32[]{:S(2)}) copy-start(s32[1,1,4]{2,1,0:T(1,128)} %param.15) | copy-start | bytes 52
  8.6 21.1 %copy-start.4 = (f32[1,1,12,1024]{3,1,2,0:T(1,128)S(1)}, f32[1,1,12,1024]{3,1,2,0:T(1,128)}, u32[]{:S(2)}) copy-start(f32[1,1,12,1024]{3,1,2,0:T(1,128)} %param.11) | copy-start | bytes 147460
  11.0 38.3 %copy-start.3 = (f32[384,192]{0,1:T(8,128)S(1)}, f32[384,192]{0,1:T(8,128)}, u32[]{:S(2)}) copy-start(f32[384,192]{0,1:T(8,128)} %param.12) | copy-start | bytes 884740
  11.1 13.6 %collective-permute-start = (f32[256,128]{0,1:T(8,128)S(1)}, f32[256,128]{0,1:T(8,128)S(1)}, u32[]{:S(2)}, u32[]{:S(2)}) collective-permute-start(f32[256,128]{0,1:T(8,128)S(1)} %get-tuple-element.9), channel_id=1, source_target_pairs={{0,1},{1,2},{2,3},{3,4},{4,5},{5,6},{6,7},{7,8},{8,9},{9,10},{10,1... | collective-permute-start | bytes 393224 | tf_op jit(solution)/shard_map/ppermute | solution.py:15
  15.3 9.4 %collective-permute-start.3 = (f32[256,128]{0,1:T(8,128)S(1)}, f32[256,128]{0,1:T(8,128)S(1)}, u32[]{:S(2)}, u32[]{:S(2)}) collective-permute-start(f32[256,128]{0,1:T(8,128)S(1)} %get-tuple-element.10), channel_id=1, source_target_pairs={{32,0},{64,32},{96,64},{128,96},{160,128},{192,160},{224,192},{256... | collective-permute-start | bytes 393224 | tf_op jit(solution)/shard_map/ppermute | solution.py:15
  21.3 3.9 %collective-permute-start.2 = (f32[256,128]{0,1:T(8,128)S(1)}, f32[256,128]{0,1:T(8,128)S(1)}, u32[]{:S(2)}, u32[]{:S(2)}) collective-permute-start(f32[256,128]{0,1:T(8,128)S(1)} %get-tuple-element.11), channel_id=1, source_target_pairs={{0,32},{32,64},{64,96},{96,128},{128,160},{160,192},{192,224},{224... | collective-permute-start | bytes 393224 | tf_op jit(solution)/shard_map/ppermute | solution.py:15
  23.3 6.5 %collective-permute-start.1 = (f32[256,128]{0,1:T(8,128)S(1)}, f32[256,128]{0,1:T(8,128)S(1)}, u32[]{:S(2)}, u32[]{:S(2)}) collective-permute-start(f32[256,128]{0,1:T(8,128)S(1)} %get-tuple-element.12), channel_id=1, source_target_pairs={{1,0},{2,1},{3,2},{4,3},{5,4},{6,5},{7,6},{8,7},{9,8},{10,9},{11,1... | collective-permute-start | bytes 393224 | tf_op jit(solution)/shard_map/ppermute | solution.py:15
  24.7 5.6 %copy-start.7 = (f32[256,128]{0,1:T(8,128)}, f32[256,128]{0,1:T(8,128)S(1)}, u32[]{:S(2)}) copy-start(f32[256,128]{0,1:T(8,128)S(1)} %collective-permute-done) | copy-start | bytes 393220
  24.7 5.7 %copy-start.9 = (f32[256,128]{0,1:T(8,128)}, f32[256,128]{0,1:T(8,128)S(1)}, u32[]{:S(2)}) copy-start(f32[256,128]{0,1:T(8,128)S(1)} %collective-permute-done.3) | copy-start | bytes 393220
  25.2 5.1 %copy-start.10 = (f32[256,128]{0,1:T(8,128)}, f32[256,128]{0,1:T(8,128)S(1)}, u32[]{:S(2)}) copy-start(f32[256,128]{0,1:T(8,128)S(1)} %collective-permute-done.2) | copy-start | bytes 393220
  29.7 0.7 copy-start.11
  50.7 75.7 %copy-start.8 = (f32[256,128]{0,1:T(8,128)S(1)}, f32[256,128]{0,1:T(8,128)}, u32[]{:S(2)}) copy-start(f32[256,128]{0,1:T(8,128)} %copy-done.7) | copy-start | bytes 393220
  87.7 185.4 %all-gather.5.cloned.1.call-start = ((), (), s32[]{:S(2)}) async-start(), calls=%async_computation.11 | async-start | bytes 3342336 | tf_op jit(solution)/shard_map/all_gather | solution.py:60
  126.5 2.8 copy-start.1
  161.2 17.7 %copy-start.5 = (f32[1,1,12,1024]{3,1,2,0:T(1,128)S(1)}, f32[1,1,12,1024]{3,1,2,0:T(1,128)}, u32[]{:S(2)}) copy-start(f32[1,1,12,1024]{3,1,2,0:T(1,128)} %param.11) | copy-start | bytes 147460
  163.7 9.3 %collective-permute-start.4 = (f32[256,128]{0,1:T(8,128)S(1)}, f32[256,128]{0,1:T(8,128)S(1)}, u32[]{:S(2)}, u32[]{:S(2)}) collective-permute-start(f32[256,128]{0,1:T(8,128)S(1)} %get-tuple-element.5), channel_id=1, source_target_pairs={{0,1},{1,2},{2,3},{3,4},{4,5},{5,6},{6,7},{7,8},{8,9},{9,10},{10,1... | collective-permute-start | bytes 393224 | tf_op jit(solution)/shard_map/ppermute | solution.py:15
  166.0 6.9 %collective-permute-start.7 = (f32[256,128]{0,1:T(8,128)S(1)}, f32[256,128]{0,1:T(8,128)S(1)}, u32[]{:S(2)}, u32[]{:S(2)}) collective-permute-start(f32[256,128]{0,1:T(8,128)S(1)} %get-tuple-element.6), channel_id=1, source_target_pairs={{32,0},{64,32},{96,64},{128,96},{160,128},{192,160},{224,192},{256... | collective-permute-start | bytes 393224 | tf_op jit(solution)/shard_map/ppermute | solution.py:15
  168.6 4.9 %collective-permute-start.6 = (f32[256,128]{0,1:T(8,128)S(1)}, f32[256,128]{0,1:T(8,128)S(1)}, u32[]{:S(2)}, u32[]{:S(2)}) collective-permute-start(f32[256,128]{0,1:T(8,128)S(1)} %get-tuple-element.7), channel_id=1, source_target_pairs={{0,32},{32,64},{64,96},{96,128},{128,160},{160,192},{192,224},{224... | collective-permute-start | bytes 393224 | tf_op jit(solution)/shard_map/ppermute | solution.py:15
  171.6 7.2 %collective-permute-start.5 = (f32[256,128]{0,1:T(8,128)S(1)}, f32[256,128]{0,1:T(8,128)S(1)}, u32[]{:S(2)}, u32[]{:S(2)}) collective-permute-start(f32[256,128]{0,1:T(8,128)S(1)} %get-tuple-element.8), channel_id=1, source_target_pairs={{1,0},{2,1},{3,2},{4,3},{5,4},{6,5},{7,6},{8,7},{9,8},{10,9},{11,1... | collective-permute-start | bytes 393224 | tf_op jit(solution)/shard_map/ppermute | solution.py:15
  172.9 6.5 %copy-start.12 = (f32[256,128]{0,1:T(8,128)}, f32[256,128]{0,1:T(8,128)S(1)}, u32[]{:S(2)}) copy-start(f32[256,128]{0,1:T(8,128)S(1)} %collective-permute-done.4) | copy-start | bytes 393220
  173.0 6.5 %copy-start.13 = (f32[256,128]{0,1:T(8,128)}, f32[256,128]{0,1:T(8,128)S(1)}, u32[]{:S(2)}) copy-start(f32[256,128]{0,1:T(8,128)S(1)} %collective-permute-done.7) | copy-start | bytes 393220
  173.6 5.9 %copy-start.14 = (f32[256,128]{0,1:T(8,128)}, f32[256,128]{0,1:T(8,128)S(1)}, u32[]{:S(2)}) copy-start(f32[256,128]{0,1:T(8,128)S(1)} %collective-permute-done.6) | copy-start | bytes 393220
  178.8 0.7 copy-start.15
  192.1 81.0 %copy-start.6 = (f32[1,1,12,1024]{3,1,2,0:T(1,128)S(1)}, f32[1,1,12,1024]{3,1,2,0:T(1,128)}, u32[]{:S(2)}) copy-start(f32[1,1,12,1024]{3,1,2,0:T(1,128)} %param.11) | copy-start | bytes 147460
  273.1 2.8 copy-start.2
Sparse Core Ops, SparseCore 0:
  87.8 38.5 all-gather.2
  234.5 38.5 all-gather.4
where the time goes:
time: 318 us; the launch traced here: 317 us
  blocking collectives  162 us (51%)
  waiting for transfers between devices  88.3 us (28%)
  starting transfers between devices  22.7 us (7%)
  matrix products  16.9 us (5%)
  between operations  13.8 us (4%)
  local copies, waits for them, and re-layouts  10.4 us (3%)
  other arithmetic  3.24 us (1%)
    all_to_all x8, blocking collectives, from_everyone(): return lax.all_to_all(copies, axis, split_axis=0, concat_axis=0, tiled=True)  123 us
    all_gather x2, waiting for transfers between devices, picked_2(): lax.all_gather(x, axis)  77.4 us
    all_to_all x2, blocking collectives, sent_and_summed(): lax.all_to_all(tiles, axis, split_axis=0, concat_axis=0, tiled=True)  38.8 us
    ppermute x8, starting transfers between devices, passed_along(): return lax.ppermute(x, axis, pairs)  22.7 us
    ppermute x8, waiting for transfers between devices, passed_along(): return lax.ppermute(x, axis, pairs)  10.9 us
  transfers between devices with their start and end apart: 10, of which 6 were waited for; matrix products, arithmetic and copies ran while one was open for 0% of the time, Pallas kernels for 0%

commit v1 on v0

v1 whole, which is shorter than its diff:
```python
import jax
import jax.numpy as jnp
from jax import lax
from jax.experimental import pallas as pl
from jax.experimental.pallas import tpu as pltpu
from jax.sharding import PartitionSpec as P

MESH = pl.DeviceIdType.MESH
F32 = jnp.float32
BF16 = jnp.bfloat16
ITERS = 2
NR = 16
NCOL = 32
M = 1024
FACE = 256
NC = 12
R = 128
LEVELS = 16


def dot(a, b):
    return jnp.dot(a, b, preferred_element_type=F32)


def split(v):
    high = v.astype(BF16)
    low = (v - high.astype(F32)).astype(BF16)
    return high, low


def kernel(
    slip_h, flex_h, schur_h, coup_h, coarse_h, table, bidx_h, frows, out_ref,
    slip, flex, schur, coup, coarse, bidx,
    bound, lam, disp, paired, jump, search, pb_v, ct, c2,
    asend, arecv, aleft, aright, ahi, alo,
    xsend, xall, part, parts, zsend, zall, psend, pall,
    load_sem, a_sem, face_s, face_r, x_sem, part_sem, z_sem, p_sem,
):
    r = lax.axis_index("row")
    c = lax.axis_index("col")

    loads = [
        pltpu.make_async_copy(coarse_h, coarse, load_sem.at[0]),
        pltpu.make_async_copy(bidx_h.at[0], bidx, load_sem.at[1]),
        pltpu.make_async_copy(slip_h.at[0, 0], slip, load_sem.at[2]),
        pltpu.make_async_copy(flex_h.at[0, 0], flex, load_sem.at[3]),
        pltpu.make_async_copy(coup_h.at[0, 0], coup, load_sem.at[4]),
        pltpu.make_async_copy(schur_h.at[0, 0], schur, load_sem.at[5]),
    ]
    for copy in loads:
        copy.start()

    xall[:, :, NC:16, :] = jnp.zeros((ITERS, NR, 16 - NC, R), F32)

    barrier = pltpu.get_barrier_semaphore()

    def greet_row(k, carry):
        pl.semaphore_signal(barrier, inc=1, device_id=(lax.rem(r + k, NR), c), device_id_type=MESH)
        return carry

    def greet_col(k, carry):
        pl.semaphore_signal(barrier, inc=1, device_id=(r, lax.rem(c + k, NCOL)), device_id_type=MESH)
        return carry

    lax.fori_loop(1, NCOL, greet_col, 0)
    lax.fori_loop(1, NR, greet_row, 0)

    loads[0].wait()
    for a in range(NR):
        lo, hi = a * NC, NR * NC + a * NC
        asend[a, 0:NC, :] = coarse[lo : lo + NC, 0:128]
        asend[a, NC : 2 * NC, :] = coarse[hi : hi + NC, 0:128]
        asend[a, 2 * NC : 3 * NC, 0:64] = coarse[lo : lo + NC, 128:192]
        asend[a, 2 * NC : 3 * NC, 64:128] = coarse[hi : hi + NC, 128:192]

    loads[1].wait()
    for q in range(M // 128):
        level = bidx[:, q * 128 : (q + 1) * 128]
        row = jnp.zeros((1, 128), F32)
        for n in range(LEVELS):
            row = jnp.where(level == n, table[n], row)
        bound[q * 128 : (q + 1) * 128, :] = jnp.transpose(jnp.broadcast_to(row, (128, 128)))

    loads[2].wait()
    lam[...] = jnp.clip(slip[...].astype(F32), -bound[...], bound[...])
    loads[3].wait()

    pl.semaphore_wait(barrier, NR + NCOL - 2)

    def send_a(k, carry):
        to = lax.rem(r + k, NR)
        pltpu.make_async_remote_copy(
            asend.at[to], arecv.at[r], a_sem.at[0], a_sem.at[1], device_id=(to, c), device_id_type=MESH
        ).start()
        return carry

    lax.fori_loop(1, NR, send_a, 0)
    arecv[r] = asend[r]

    loads[4].wait()
    coup_hi, coup_lo = split(coup[...])
    c2[0:NC, :] = coup_hi.astype(F32)
    c2[NC:16, :] = jnp.zeros((4, M), F32)
    c2[16 : 16 + NC, :] = coup_lo.astype(F32)
    c2[16 + NC : 32, :] = jnp.zeros((4, M), F32)
    stacked = jnp.concatenate([c2[...], c2[0:16, :], jnp.zeros((80, M), F32)], axis=0)
    for q in range(M // 128):
        ct[q * 128 : (q + 1) * 128, :] = jnp.transpose(stacked[:, q * 128 : (q + 1) * 128]).astype(BF16)
    loads[5].wait()

    up_col, down_col = lax.rem(c + 1, NCOL), lax.rem(c + NCOL - 1, NCOL)
    up_row, down_row = lax.rem(r + 1, NR), lax.rem(r + NR - 1, NR)
    faces = (
        (1, (r, up_col), 0),
        (0, (r, down_col), 1),
        (3, (up_row, c), 2),
        (2, (down_row, c), 3),
    )

    def unpack_a():
        pltpu.make_async_copy(arecv.at[pl.ds(0, NR - 1)], arecv.at[pl.ds(0, NR - 1)], a_sem.at[1]).wait()
        lane = lax.broadcasted_iota(jnp.int32, (NC, 128), 1)
        zero = jnp.zeros((NC, 128), F32)
        for s in range(NR):
            last = arecv[s, 2 * NC : 3 * NC, :]
            aleft[2 * s, 0:NC, :] = arecv[s, 0:NC, :]
            aleft[2 * s + 1, 0:NC, :] = arecv[s, NC : 2 * NC, :]
            aright[2 * s, 0:NC, :] = jnp.where(lane < 64, last, zero)
            aright[2 * s + 1, 0:NC, :] = jnp.where(lane < 64, zero, last)
        i0 = lax.broadcasted_iota(jnp.int32, (128, 256), 0)
        i1 = lax.broadcasted_iota(jnp.int32, (128, 256), 1)
        index = jnp.where(i1 % 16 < NC, (i1 // 16) * NC + i1 % 16, -1)
        pick_left = (index == i0).astype(F32).astype(BF16)
        pick_right = (index == 128 + i0 % 64).astype(F32).astype(BF16)
        left_hi, left_lo = split(aleft[...].reshape(512, 128))
        right_hi, right_lo = split(aright[...].reshape(512, 128))
        ahi[...] = (dot(left_hi, pick_left) + dot(right_hi, pick_right)).astype(BF16)
        alo[...] = (dot(left_lo, pick_left) + dot(right_lo, pick_right)).astype(BF16)

    aleft[...] = jnp.zeros_like(aleft)
    aright[...] = jnp.zeros_like(aright)

    for it in range(ITERS):
        lam_b = lam[...].astype(BF16)
        for own, to, there in faces:
            rows = slice(own * FACE, (own + 1) * FACE)
            disp[it, rows, :] = dot(flex[rows, :], lam_b)
            pltpu.make_async_remote_copy(
                disp.at[it, pl.ds(own * FACE, FACE)],
                paired.at[it, pl.ds(there * FACE, FACE)],
                face_s.at[it, own],
                face_r.at[it, there],
                device_id=to,
                device_id_type=MESH,
            ).start()
        for f in range(4):
            rows = slice(f * FACE, (f + 1) * FACE)
            landed = paired.at[it, pl.ds(f * FACE, FACE)]
            pltpu.make_async_copy(landed, landed, face_r.at[it, f]).wait()
            live = lax.broadcasted_iota(jnp.int32, (FACE, R), 0) < frows[0, 0, f]
            gap = disp[it, rows, :] - paired[it, rows, :] - slip[rows, :].astype(F32)
            jump[rows, :] = jnp.where(live, gap, 0.0)
        jump_hi, jump_lo = split(jump[...])
        force = dot(c2[...].astype(BF16), jnp.concatenate([jump_hi, jump_lo], axis=1))
        force = force[0:16, 0:R] + (force[0:16, R : 2 * R] + force[16:32, 0:R])
        xsend[it] = force[0:NC, :]
        xall[it, r, 0:NC, :] = force[0:NC, :]

        def send_x(k, carry):
            to = lax.rem(r + k, NR)
            pltpu.make_async_remote_copy(
                xsend.at[it], xall.at[it, r, pl.ds(0, NC)], x_sem.at[it, 0], x_sem.at[it, 1],
                device_id=(to, c), device_id_type=MESH,
            ).start()
            return carry

        lax.fori_loop(1, NR, send_x, 0)
        if it == 0:
            unpack_a()
        landed = xall.at[it, pl.ds(0, NR - 1), pl.ds(0, NC)]
        pltpu.make_async_copy(landed, landed, x_sem.at[it, 1]).wait()
        x_hi, x_lo = split(xall[it].reshape(256, R))
        both = dot(ahi[...], jnp.concatenate([x_hi, x_lo], axis=1))
        sums = both[:, 0:R] + (both[:, R : 2 * R] + dot(alo[...], x_hi))
        part[it] = sums.reshape(NCOL, 16, R)[:, 0:NC, :]
        parts[it, c] = part[it, c]

        def send_part(k, carry):
            to = lax.rem(c + k, NCOL)
            pltpu.make_async_remote_copy(
                part.at[it, to], parts.at[it, c], part_sem.at[it, 0], part_sem.at[it, 1],
                device_id=(r, to), device_id_type=MESH,
            ).start()
            return carry

        lax.fori_loop(1, NCOL, send_part, 0)
        landed = parts.at[it, pl.ds(0, NCOL - 1)]
        pltpu.make_async_copy(landed, landed, part_sem.at[it, 1]).wait()
        values = jnp.sum(parts[it], axis=0)
        values = jnp.concatenate([values, jnp.zeros((4, R), F32)], axis=0)
        v_hi, v_lo = split(values)
        v_hi, v_lo = v_hi.astype(F32), v_lo.astype(F32)
        stack = jnp.concatenate([v_hi, v_hi, v_lo, jnp.zeros((80, R), F32)], axis=0).astype(BF16)
        p_b = (jump[...] - dot(ct[...], stack)).astype(BF16)
        gain = jnp.zeros((1, R), F32)
        pb_v[...] = p_b
        for f in range(4):
            rows = slice(f * FACE, (f + 1) * FACE)
            s = dot(schur[rows, :], p_b)
            search[rows, :] = s
            gain = gain + jnp.sum(pb_v[rows, :].astype(F32) * s, axis=0, keepdims=True)
        s_b = search[...].astype(BF16)
        curve = jnp.zeros((1, R), F32)
        for f in range(4):
            rows = slice(f * FACE, (f + 1) * FACE)
            curve = curve + jnp.sum(
                search[rows, :].astype(BF16).astype(F32) * dot(flex[rows, :], s_b), axis=0, keepdims=True
            )
        both = jnp.concatenate([gain, curve], axis=0)
        zsend[it] = both
        zall[it, r] = both

        def send_z(k, carry):
            to = lax.rem(r + k, NR)
            pltpu.make_async_remote_copy(
                zsend.at[it], zall.at[it, r], z_sem.at[it, 0], z_sem.at[it, 1],
                device_id=(to, c), device_id_type=MESH,
            ).start()
            return carry

        lax.fori_loop(1, NR, send_z, 0)
        landed = zall.at[it, pl.ds(0, NR - 1)]
        pltpu.make_async_copy(landed, landed, z_sem.at[it, 1]).wait()
        both = jnp.sum(zall[it], axis=0)
        psend[it] = both
        pall[it, c] = both

        def send_p(k, carry):
            to = lax.rem(c + k, NCOL)
            pltpu.make_async_remote_copy(
                psend.at[it], pall.at[it, c], p_sem.at[it, 0], p_sem.at[it, 1],
                device_id=(r, to), device_id_type=MESH,
            ).start()
            return carry

        lax.fori_loop(1, NCOL, send_p, 0)
        landed = pall.at[it, pl.ds(0, NCOL - 1)]
        pltpu.make_async_copy(landed, landed, p_sem.at[it, 1]).wait()
        both = jnp.sum(pall[it], axis=0)
        step = both[0:1, :] / both[1:2, :]
        moved = jnp.clip(lam[...] - step * search[...], -bound[...], bound[...])
        if it < ITERS - 1:
            lam[...] = moved
        else:
            out_ref[...] = moved.astype(BF16)

    sent = asend.at[pl.ds(0, NR - 1)]
    pltpu.make_async_copy(sent, sent, a_sem.at[0]).wait()
    for it in range(ITERS):
        for f in range(4):
            sent = disp.at[it, pl.ds(f * FACE, FACE)]
            pltpu.make_async_copy(sent, sent, face_s.at[it, f]).wait()
        sent = xall.at[it, pl.ds(0, NR - 1), pl.ds(0, NC)]
        pltpu.make_async_copy(sent, sent, x_sem.at[it, 0]).wait()
        sent = parts.at[it, pl.ds(0, NCOL - 1)]
        pltpu.make_async_copy(sent, sent, part_sem.at[it, 0]).wait()
        sent = zall.at[it, pl.ds(0, NR - 1)]
        pltpu.make_async_copy(sent, sent, z_sem.at[it, 0]).wait()
        sent = pall.at[it, pl.ds(0, NCOL - 1)]
        pltpu.make_async_copy(sent, sent, p_sem.at[it, 0]).wait()


def local(*args):
    hbm = pl.BlockSpec(memory_space=pl.ANY)
    smem = pl.BlockSpec(memory_space=pltpu.SMEM)
    dma = pltpu.SemaphoreType.DMA
    v = pltpu.VMEM
    out = pl.pallas_call(
        kernel,
        out_shape=jax.ShapeDtypeStruct((M, R), BF16),
        in_specs=[hbm, hbm, hbm, hbm, hbm, smem, hbm, smem],
        out_specs=pl.BlockSpec(memory_space=pltpu.VMEM),
        scratch_shapes=[
            v((M, R), BF16),
            v((M, M), BF16),
            v((M, M), BF16),
            v((NC, M), F32),
            v((2 * NR * NC, NR * NC), F32),
            v((1, M), jnp.int32),
            v((M, R), F32),
            v((M, R), F32),
            v((ITERS, M, R), F32),
            v((ITERS, M, R), F32),
            v((M, R), F32),
            v((M, R), F32),
            v((M, R), BF16),
            v((M, 128), BF16),
            v((32, M), F32),
            v((NR, 3 * NC, 128), F32),
            v((NR, 3 * NC, 128), F32),
            v((NCOL, 16, 128), F32),
            v((NCOL, 16, 128), F32),
            v((512, 256), BF16),
            v((512, 256), BF16),
            v((ITERS, NC, R), F32),
            v((ITERS, NR, 16, R), F32),
            v((ITERS, NCOL, NC, R), F32),
            v((ITERS, NCOL, NC, R), F32),
            v((ITERS, 2, R), F32),
            v((ITERS, NR, 2, R), F32),
            v((ITERS, 2, R), F32),
            v((ITERS, NCOL, 2, R), F32),
            dma((6,)),
            dma((2,)),
            dma((ITERS, 4)),
            dma((ITERS, 4)),
            dma((ITERS, 2)),
            dma((ITERS, 2)),
            dma((ITERS, 2)),
            dma((ITERS, 2)),
        ],
        compiler_params=pltpu.CompilerParams(
            collective_id=0, has_side_effects=True, vmem_limit_bytes=40 * 1024 * 1024
        ),
        name="feti",
    )(*args)
    return out[None, None]


def solution(mesh):
    cell = P("row", "col", None, None)
    placed = (cell, cell, cell, cell, P("row", "col"), P(), P("row", "col", None), P("row", "col", None))
    return jax.shard_map(local, mesh=mesh, in_specs=placed, out_specs=cell, check_vma=False)
```

time: 318 us -> 94.9 us (0.30)
  blocking collectives: 162 us -> 0 us
  waiting for transfers between devices: 88.3 us -> 0 us
  Pallas kernels: 0 us -> 85.8 us
  starting transfers between devices: 22.7 us -> 0 us
  matrix products: 16.9 us -> 0 us
  between operations: 13.8 us -> 0.03 us
  other arithmetic: 3.24 us -> 0 us
    all_to_all x10 -> x0, blocking collectives: 162 us -> none  [the longest x8 123 us: from_everyone(): return lax.all_to_all(copies, axis, split_axis=0, concat_axis=0, tiled=True)]
    pallas_call x0 -> x1, Pallas kernels: none -> 85.8 us  [local(): pl.pallas_call(kernel, out_shape=jax.ShapeDtypeStruct((M, R), BF16), in_s...]
    all_gather x2 -> x0, waiting for transfers between devices: 77.4 us -> none  [picked_2(): lax.all_gather(x, axis)]
    ppermute x8 -> x0, starting transfers between devices: 22.7 us -> none  [passed_along(): return lax.ppermute(x, axis, pairs)]
    dot_general x12 -> x0, matrix products: 16.9 us -> none  [the longest x2 4.87 us: local(): jnp.dot(flex_block, lam.astype(jnp.bfloat16), preferred_element_type=jnp....]
    ppermute x8 -> x0, waiting for transfers between devices: 10.9 us -> none  [passed_along(): return lax.ppermute(x, axis, pairs)]
    unnamed x36 -> x15, local copies, waits for them, and re-layouts: 1.24 us -> 8.76 us
  transfers between devices with their start and end apart: 10 -> 0, of which waited for: 6 -> 0; matrix products, arithmetic and copies ran while one was open for 0% -> 0% of each run, Pallas kernels for 0% -> 0%
where the time goes in v1:
time: 94.9 us; the launch traced here: 94.6 us
  Pallas kernels  85.8 us (90%)
  local copies, waits for them, and re-layouts  8.76 us (9%)
    pallas_call x1, Pallas kernels, local(): pl.pallas_call(kernel, out_shape=jax.ShapeDtypeStruct((M, R), BF16), in_s...  85.8 us
    unnamed x15, local copies, waits for them, and re-layouts  8.76 us

profile of v1, /device:TPU:1, one launch (start us, length us, event | category | flops | bytes accessed | tf_op | source)
XLA Modules:
  0.0 94.6 jit_solution(16085292548417795882)
XLA Ops:
  0.0 0.8 copy.9.coup_h
  0.8 1.1 %copy.10.coarse_h = f32[384,192]{1,0:T(8,128)S(1)} copy(f32[384,192]{0,1:T(8,128)} %param.12) | data formatting | bytes 589824 | tf_op args[4]
  1.9 0.0 copy-start
  2.0 1.6 %copy-done = bf16[1,1,1024,1024]{3,2,1,0:T(8,128)(2,1)S(1)} copy-done((bf16[1,1,1024,1024]{3,2,1,0:T(8,128)(2,1)S(1)}, bf16[1,1,1024,1024]{3,2,1,0:T(8,128)(2,1)}, u32[]{:S(2)}) %copy-start) | copy-done | bytes 2097176
  3.5 0.0 copy-start.1
  3.5 1.6 %copy-done.1 = bf16[1,1,1024,1024]{3,2,1,0:T(8,128)(2,1)S(1)} copy-done((bf16[1,1,1024,1024]{3,2,1,0:T(8,128)(2,1)S(1)}, bf16[1,1,1024,1024]{3,2,1,0:T(8,128)(2,1)}, u32[]{:S(2)}) %copy-start.1) | copy-done | bytes 2097176
  5.1 0.0 copy-start.2
  5.1 0.9 %copy-done.2 = bf16[1,1,1024,128]{3,2,1,0:T(8,128)(2,1)S(1)} copy-done((bf16[1,1,1024,128]{3,2,1,0:T(8,128)(2,1)S(1)}, bf16[1,1,1024,128]{3,2,1,0:T(8,128)(2,1)}, u32[]{:S(2)}) %copy-start.2) | copy-done | bytes 262168
  6.1 0.0 copy-start.3
  6.1 0.7 copy-done.3
  6.8 0.0 copy-start.4
  6.8 0.7 copy-done.4
  7.4 0.0 copy-start.5
  7.4 0.7 copy-done.5
  8.1 85.8 %feti.1 = bf16[1024,128]{1,0:T(8,128)(2,1)S(1)} custom-call(bf16[1,1,1024,128]{3,2,1,0:T(8,128)(2,1)S(1)} %copy-done.2, bf16[1,1,1024,1024]{3,2,1,0:T(8,128)(2,1)S(1)} %copy-done, bf16[1,1,1024,1024]{3,2,1,0:T(8,128)(2,1)S(1)} %copy-done.1, f32[1,1,12,1024]{3,2,1,0:T(8,128)S(1)} %copy.9.coup_h, f32[384,192]{1,0:T(8,128)S(1)} %copy.10.coarse_h, ...), custom_call_target="tpu_custom_call" | custom-call | tf_op jit(solution)/shard_map/feti/pallas_call | solution.py:278
  93.9 0.7 copy.12
Async XLA Ops:
  1.9 1.6 %copy-start = (bf16[1,1,1024,1024]{3,2,1,0:T(8,128)(2,1)S(1)}, bf16[1,1,1024,1024]{3,2,1,0:T(8,128)(2,1)}, u32[]{:S(2)}) copy-start(bf16[1,1,1024,1024]{3,2,1,0:T(8,128)(2,1)} %flex_h.1) | copy-start | bytes 6291460
  3.5 1.6 %copy-start.1 = (bf16[1,1,1024,1024]{3,2,1,0:T(8,128)(2,1)S(1)}, bf16[1,1,1024,1024]{3,2,1,0:T(8,128)(2,1)}, u32[]{:S(2)}) copy-start(bf16[1,1,1024,1024]{3,2,1,0:T(8,128)(2,1)} %schur_h.1) | copy-start | bytes 6291460
  5.1 0.9 %copy-start.2 = (bf16[1,1,1024,128]{3,2,1,0:T(8,128)(2,1)S(1)}, bf16[1,1,1024,128]{3,2,1,0:T(8,128)(2,1)}, u32[]{:S(2)}) copy-start(bf16[1,1,1024,128]{3,2,1,0:T(8,128)(2,1)} %slip_h.1) | copy-start | bytes 786436
  6.1 0.7 copy-start.3
  6.8 0.7 copy-start.4
  7.4 0.7 copy-start.5

commit v2 on v1

v2 whole, which is shorter than its diff:
```python
import jax
import jax.numpy as jnp
from jax import lax
from jax.experimental import pallas as pl
from jax.experimental.pallas import tpu as pltpu
from jax.sharding import PartitionSpec as P

MESH = pl.DeviceIdType.MESH
F32 = jnp.float32
BF16 = jnp.bfloat16
ITERS = 2
NR = 16
NCOL = 32
M = 1024
FACE = 256
NC = 12
R = 128
LEVELS = 16


def dot(a, b):
    return jnp.dot(a, b, preferred_element_type=F32)


def split(v):
    high = v.astype(BF16)
    low = (v - high.astype(F32)).astype(BF16)
    return high, low


def swing(m):
    return 4 + (1 - 2 * lax.rem(m, 2)) * ((m + 1) // 2)


def each_in_row(r, act):
    z, core = r // 2, lax.rem(r, 2)

    def step(m, carry):
        at = lax.rem(z + swing(m), 8) * 2
        act(at + core)
        act(at + 1 - core)
        return carry

    lax.fori_loop(0, 7, step, 0)
    act(z * 2 + 1 - core)


def each_in_col(c, act):
    x, y = c // 8, lax.rem(c, 8)

    def step(m, carry):
        at = lax.rem(y + swing(m), 8)
        for dx in (2, 1, 3, 0):
            act(lax.rem(x + dx, 4) * 8 + at)
        return carry

    lax.fori_loop(0, 7, step, 0)
    for dx in (2, 1, 3):
        act(lax.rem(x + dx, 4) * 8 + y)


def kernel(
    slip_h, flex_h, schur_h, coup_h, coarse_h, table_h, bidx_h, frows_h, out_ref,
    slip, flex, schur, coup, turned, coarse, bidx, table, frows,
    bound, lam, disp, paired, jump, search, pb_v, ct, c2, cfull, cl, cl_in, g2, fixed, wsend, w_in,
    asend, arecv, aleft, aright, ahi, alo,
    xsend, xall, part, parts, zsend, zall, psend, pall,
    load_sem, a_sem, face_s, face_r, cl_s, cl_r, w_s, w_r, x_sem, part_sem, z_sem, p_sem,
):
    r = lax.axis_index("row")
    c = lax.axis_index("col")

    load_table = pltpu.make_async_copy(table_h, table, load_sem.at[0])
    load_bidx = pltpu.make_async_copy(bidx_h.at[0], bidx, load_sem.at[1])
    load_slip = pltpu.make_async_copy(slip_h.at[0, 0], slip, load_sem.at[2])
    load_flex = pltpu.make_async_copy(flex_h.at[0, 0], flex, load_sem.at[3])
    load_frows = pltpu.make_async_copy(frows_h.at[0], frows, load_sem.at[4])
    load_coup = pltpu.make_async_copy(coup_h, coup, load_sem.at[5])
    load_coarse = pltpu.make_async_copy(coarse_h, turned.at[pl.ds(0, NR * NC)], load_sem.at[6])
    load_schur = pltpu.make_async_copy(schur_h.at[0, 0], schur, load_sem.at[7])
    loads = (
        load_table, load_bidx, load_slip, load_flex, load_frows, load_coup, load_coarse, load_schur
    )
    for copy in loads:
        copy.start()

    xall[:, :, NC:16, :] = jnp.zeros((ITERS, NR, 16 - NC, R), F32)

    barrier = pltpu.get_barrier_semaphore()

    def greet(to):
        pl.semaphore_signal(barrier, inc=1, device_id=to, device_id_type=MESH)

    each_in_col(c, lambda to: greet((r, to)))
    each_in_row(r, lambda to: greet((to, c)))

    load_table.wait()
    load_bidx.wait()
    for q in range(M // 128):
        level = bidx[:, q * 128 : (q + 1) * 128]
        row = jnp.zeros((1, 128), F32)
        for n in range(LEVELS):
            row = jnp.where(level == n, table[n], row)
        bound[q * 128 : (q + 1) * 128, :] = jnp.transpose(jnp.broadcast_to(row, (128, 128)))

    load_slip.wait()
    lam[...] = jnp.clip(slip[...].astype(F32), -bound[...], bound[...])

    up_col, down_col = lax.rem(c + 1, NCOL), lax.rem(c + NCOL - 1, NCOL)
    up_row, down_row = lax.rem(r + 1, NR), lax.rem(r + NR - 1, NR)
    faces = (
        (1, (r, up_col), 0),
        (0, (r, down_col), 1),
        (3, (up_row, c), 2),
        (2, (down_row, c), 3),
    )

    def displace(it, own):
        rows = slice(own * FACE, (own + 1) * FACE)
        disp[it, rows, :] = dot(flex[rows, :], lam[...].astype(BF16))

    def send_face(it, own, to, there):
        pltpu.make_async_remote_copy(
            disp.at[it, pl.ds(own * FACE, FACE)],
            paired.at[it, pl.ds(there * FACE, FACE)],
            face_s.at[it, own],
            face_r.at[it, there],
            device_id=to,
            device_id_type=MESH,
        ).start()

    def find_jump(it):
        for f in range(4):
            rows = slice(f * FACE, (f + 1) * FACE)
            landed = paired.at[it, pl.ds(f * FACE, FACE)]
            pltpu.make_async_copy(landed, landed, face_r.at[it, f]).wait()
            live = lax.broadcasted_iota(jnp.int32, (FACE, R), 0) < frows[0, f]
            gap = disp[it, rows, :] - paired[it, rows, :] - slip[rows, :].astype(F32)
            jump[rows, :] = jnp.where(live, gap, 0.0)

    load_flex.wait()
    for own, to, there in faces:
        displace(0, own)
    pl.semaphore_wait(barrier, NR + NCOL - 2)
    for own, to, there in faces:
        send_face(0, own, to, there)

    load_coarse.wait()
    for i in range(2):
        for j in range(3):
            coarse[j * 128 : (j + 1) * 128, i * 128 : (i + 1) * 128] = jnp.transpose(
                turned[i * 128 : (i + 1) * 128, j * 128 : (j + 1) * 128]
            )
    for a in range(NR):
        lo, hi = a * NC, NR * NC + a * NC
        asend[a, 0:NC, :] = coarse[lo : lo + NC, 0:128]
        asend[a, NC : 2 * NC, :] = coarse[hi : hi + NC, 0:128]
        asend[a, 2 * NC : 3 * NC, 0:64] = coarse[lo : lo + NC, 128:192]
        asend[a, 2 * NC : 3 * NC, 64:128] = coarse[hi : hi + NC, 128:192]

    def send_a(to):
        pltpu.make_async_remote_copy(
            asend.at[to], arecv.at[r], a_sem.at[0], a_sem.at[1], device_id=(to, c), device_id_type=MESH
        ).start()

    each_in_row(r, send_a)
    arecv[r] = asend[r]

    load_coup.wait()
    load_frows.wait()
    for k in range(NC):
        cfull[k : k + 1, :] = coup[k]
    cfull[NC:16, :] = jnp.zeros((4, M), F32)
    coup_hi, coup_lo = split(cfull[...])
    c2[0:16, :] = coup_hi.astype(F32)
    c2[16:32, :] = coup_lo.astype(F32)
    stacked = jnp.concatenate([c2[...], c2[0:16, :], jnp.zeros((80, M), F32)], axis=0)
    for q in range(M // 128):
        ct[q * 128 : (q + 1) * 128, :] = jnp.transpose(stacked[:, q * 128 : (q + 1) * 128]).astype(BF16)
    for f in range(4):
        live = lax.broadcasted_iota(jnp.int32, (16, FACE), 1) < frows[0, f]
        cl[f] = jnp.where(live, cfull[:, f * FACE : (f + 1) * FACE], 0.0)
    for own, to, there in faces:
        pltpu.make_async_remote_copy(
            cl.at[own], cl_in.at[there], cl_s.at[own], cl_r.at[there], device_id=to, device_id_type=MESH
        ).start()
    load_schur.wait()

    def to_bf16_rows(hi, lo):
        return jnp.concatenate([hi.astype(F32), lo.astype(F32)], axis=0).astype(BF16)

    def fold_flex():
        total = jnp.zeros((32, M), F32)
        fix = jnp.zeros((32, R), F32)
        for f in range(4):
            rows = slice(f * FACE, (f + 1) * FACE)
            landed = cl_in.at[f]
            pltpu.make_async_copy(landed, landed, cl_r.at[f]).wait()
            own = to_bf16_rows(*split(cl[f]))
            total = total + dot(own, flex[rows, :])
            fix = fix + dot(own, slip[rows, :])
            across = dot(to_bf16_rows(*split(cl_in[f])), flex[rows, :])
            hi, lo = split(across[0:16] + across[16:32])
            g2[16 + 16 * f : 32 + 16 * f, :] = hi
            g2[96 + 16 * f : 112 + 16 * f, :] = lo
        hi, lo = split(total[0:16] + total[16:32])
        g2[0:16, :] = hi
        g2[80:96, :] = lo
        fixed[...] = fix[0:16] + fix[16:32]

    def unpack_a():
        pltpu.make_async_copy(arecv.at[pl.ds(0, NR - 1)], arecv.at[pl.ds(0, NR - 1)], a_sem.at[1]).wait()
        lane = lax.broadcasted_iota(jnp.int32, (NC, 128), 1)
        zero = jnp.zeros((NC, 128), F32)
        for s in range(NR):
            last = arecv[s, 2 * NC : 3 * NC, :]
            aleft[2 * s, 0:NC, :] = arecv[s, 0:NC, :]
            aleft[2 * s + 1, 0:NC, :] = arecv[s, NC : 2 * NC, :]
            aright[2 * s, 0:NC, :] = jnp.where(lane < 64, last, zero)
            aright[2 * s + 1, 0:NC, :] = jnp.where(lane < 64, zero, last)
        i0 = lax.broadcasted_iota(jnp.int32, (128, 256), 0)
        i1 = lax.broadcasted_iota(jnp.int32, (128, 256), 1)
        index = jnp.where(i1 % 16 < NC, (i1 // 16) * NC + i1 % 16, -1)
        pick_left = (index == i0).astype(F32).astype(BF16)
        pick_right = (index == 128 + i0 % 64).astype(F32).astype(BF16)
        left_hi, left_lo = split(aleft[...].reshape(512, 128))
        right_hi, right_lo = split(aright[...].reshape(512, 128))
        ahi[...] = (dot(left_hi, pick_left) + dot(right_hi, pick_right)).astype(BF16)
        alo[...] = (dot(left_lo, pick_left) + dot(right_lo, pick_right)).astype(BF16)

    aleft[...] = jnp.zeros_like(aleft)
    aright[...] = jnp.zeros_like(aright)

    for it in range(ITERS):
        if it == 0:
            find_jump(it)
            jump_hi, jump_lo = split(jump[...])
            force = dot(c2[...].astype(BF16), jnp.concatenate([jump_hi, jump_lo], axis=1))
            force = force[0:16, 0:R] + (force[0:16, R : 2 * R] + force[16:32, 0:R])
        else:
            adds = dot(g2[...], lam[...].astype(BF16))
            adds = adds[0:80] + adds[80:160]
            for own, to, there in faces:
                wsend[own] = adds[16 + 16 * own : 16 + 16 * own + NC]
                pltpu.make_async_remote_copy(
                    wsend.at[own], w_in.at[there], w_s.at[own], w_r.at[there], device_id=to, device_id_type=MESH
                ).start()
            for own, to, there in faces:
                displace(it, own)
                send_face(it, own, to, there)
            force = adds[0:NC] - fixed[0:NC, :]
            for f in range(4):
                landed = w_in.at[f]
                pltpu.make_async_copy(landed, landed, w_r.at[f]).wait()
                force = force - w_in[f]
        xsend[it] = force[0:NC, :]
        xall[it, r, 0:NC, :] = force[0:NC, :]

        def send_x(to):
            pltpu.make_async_remote_copy(
                xsend.at[it], xall.at[it, r, pl.ds(0, NC)], x_sem.at[it, 0], x_sem.at[it, 1],
                device_id=(to, c), device_id_type=MESH,
            ).start()

        each_in_row(r, send_x)
        if it == 0:
            unpack_a()
        landed = xall.at[it, pl.ds(0, NR - 1), pl.ds(0, NC)]
        pltpu.make_async_copy(landed, landed, x_sem.at[it, 1]).wait()
        x_hi, x_lo = split(xall[it].reshape(256, R))
        both = dot(ahi[...], jnp.concatenate([x_hi, x_lo], axis=1))
        sums = both[:, 0:R] + (both[:, R : 2 * R] + dot(alo[...], x_hi))
        part[it] = sums.reshape(NCOL, 16, R)[:, 0:NC, :]
        parts[it, c] = part[it, c]

        def send_part(to):
            pltpu.make_async_remote_copy(
                part.at[it, to], parts.at[it, c], part_sem.at[it, 0], part_sem.at[it, 1],
                device_id=(r, to), device_id_type=MESH,
            ).start()

        each_in_col(c, send_part)
        if it == 0:
            fold_flex()
        else:
            find_jump(it)
        landed = parts.at[it, pl.ds(0, NCOL - 1)]
        pltpu.make_async_copy(landed, landed, part_sem.at[it, 1]).wait()
        values = jnp.sum(parts[it], axis=0)
        values = jnp.concatenate([values, jnp.zeros((4, R), F32)], axis=0)
        v_hi, v_lo = split(values)
        v_hi, v_lo = v_hi.astype(F32), v_lo.astype(F32)
        stack = jnp.concatenate([v_hi, v_hi, v_lo, jnp.zeros((80, R), F32)], axis=0).astype(BF16)
        p_b = (jump[...] - dot(ct[...], stack)).astype(BF16)
        gain = jnp.zeros((1, R), F32)
        pb_v[...] = p_b
        for f in range(4):
            rows = slice(f * FACE, (f + 1) * FACE)
            s = dot(schur[rows, :], p_b)
            search[rows, :] = s
            gain = gain + jnp.sum(pb_v[rows, :].astype(F32) * s, axis=0, keepdims=True)
        s_b = search[...].astype(BF16)
        curve = jnp.zeros((1, R), F32)
        for f in range(4):
            rows = slice(f * FACE, (f + 1) * FACE)
            curve = curve + jnp.sum(
                search[rows, :].astype(BF16).astype(F32) * dot(flex[rows, :], s_b), axis=0, keepdims=True
            )
        both = jnp.concatenate([gain, curve], axis=0)
        zsend[it] = both
        zall[it, r] = both

        def send_z(to):
            pltpu.make_async_remote_copy(
                zsend.at[it], zall.at[it, r], z_sem.at[it, 0], z_sem.at[it, 1],
                device_id=(to, c), device_id_type=MESH,
            ).start()

        each_in_row(r, send_z)
        landed = zall.at[it, pl.ds(0, NR - 1)]
        pltpu.make_async_copy(landed, landed, z_sem.at[it, 1]).wait()
        both = jnp.sum(zall[it], axis=0)
        psend[it] = both
        pall[it, c] = both

        def send_p(to):
            pltpu.make_async_remote_copy(
                psend.at[it], pall.at[it, c], p_sem.at[it, 0], p_sem.at[it, 1],
                device_id=(r, to), device_id_type=MESH,
            ).start()

        each_in_col(c, send_p)
        landed = pall.at[it, pl.ds(0, NCOL - 1)]
        pltpu.make_async_copy(landed, landed, p_sem.at[it, 1]).wait()
        both = jnp.sum(pall[it], axis=0)
        step = both[0:1, :] / both[1:2, :]
        moved = jnp.clip(lam[...] - step * search[...], -bound[...], bound[...])
        if it < ITERS - 1:
            lam[...] = moved
        else:
            out_ref[...] = moved.astype(BF16)

    sent = asend.at[pl.ds(0, NR - 1)]
    pltpu.make_async_copy(sent, sent, a_sem.at[0]).wait()
    for f in range(4):
        pltpu.make_async_copy(cl.at[f], cl.at[f], cl_s.at[f]).wait()
        pltpu.make_async_copy(wsend.at[f], wsend.at[f], w_s.at[f]).wait()
    for it in range(ITERS):
        for f in range(4):
            sent = disp.at[it, pl.ds(f * FACE, FACE)]
            pltpu.make_async_copy(sent, sent, face_s.at[it, f]).wait()
        sent = xall.at[it, pl.ds(0, NR - 1), pl.ds(0, NC)]
        pltpu.make_async_copy(sent, sent, x_sem.at[it, 0]).wait()
        sent = parts.at[it, pl.ds(0, NCOL - 1)]
        pltpu.make_async_copy(sent, sent, part_sem.at[it, 0]).wait()
        sent = zall.at[it, pl.ds(0, NR - 1)]
        pltpu.make_async_copy(sent, sent, z_sem.at[it, 0]).wait()
        sent = pall.at[it, pl.ds(0, NCOL - 1)]
        pltpu.make_async_copy(sent, sent, p_sem.at[it, 0]).wait()


def local(slip_load, flexibility, schur, corner_coupling, coarse_inverse, bounds_table, bound_index, face_rows):
    hbm = pl.BlockSpec(memory_space=pl.ANY)
    dma = pltpu.SemaphoreType.DMA
    v = pltpu.VMEM
    out = pl.pallas_call(
        kernel,
        out_shape=pltpu.VMEM((M, R), BF16),
        in_specs=[hbm] * 8,
        out_specs=pl.BlockSpec(memory_space=pltpu.VMEM),
        scratch_shapes=[
            v((M, R), BF16),
            v((M, M), BF16),
            v((M, M), BF16),
            v((NC, 1, M), F32),
            v((256, 2 * NR * NC), F32),
            v((2 * NR * NC, 256), F32),
            v((1, M), jnp.int32),
            pltpu.SMEM((LEVELS,), F32),
            pltpu.SMEM((1, 4), jnp.int32),
            v((M, R), F32),
            v((M, R), F32),
            v((ITERS, M, R), F32),
            v((ITERS, M, R), F32),
            v((M, R), F32),
            v((M, R), F32),
            v((M, R), BF16),
            v((M, 128), BF16),
            v((32, M), F32),
            v((16, M), F32),
            v((4, 16, FACE), F32),
            v((4, 16, FACE), F32),
            v((160, M), BF16),
            v((16, R), F32),
            v((4, NC, R), F32),
            v((4, NC, R), F32),
            v((NR, 3 * NC, 128), F32),
            v((NR, 3 * NC, 128), F32),
            v((NCOL, 16, 128), F32),
            v((NCOL, 16, 128), F32),
            v((512, 256), BF16),
            v((512, 256), BF16),
            v((ITERS, NC, R), F32),
            v((ITERS, NR, 16, R), F32),
            v((ITERS, NCOL, NC, R), F32),
            v((ITERS, NCOL, NC, R), F32),
            v((ITERS, 2, R), F32),
            v((ITERS, NR, 2, R), F32),
            v((ITERS, 2, R), F32),
            v((ITERS, NCOL, 2, R), F32),
            dma((8,)),
            dma((2,)),
            dma((ITERS, 4)),
            dma((ITERS, 4)),
            dma((4,)),
            dma((4,)),
            dma((4,)),
            dma((4,)),
            dma((ITERS, 2)),
            dma((ITERS, 2)),
            dma((ITERS, 2)),
            dma((ITERS, 2)),
        ],
        compiler_params=pltpu.CompilerParams(
            collective_id=0, has_side_effects=True, vmem_limit_bytes=56 * 1024 * 1024
        ),
        name="feti",
    )(
        slip_load, flexibility, schur, corner_coupling.reshape(NC, 1, M), coarse_inverse.T,
        bounds_table, bound_index, face_rows,
    )
    return out[None, None]


def solution(mesh):
    cell = P("row", "col", None, None)
    placed = (cell, cell, cell, cell, P("row", "col"), P(), P("row", "col", None), P("row", "col", None))
    return jax.shard_map(local, mesh=mesh, in_specs=placed, out_specs=cell, check_vma=False)
```

time: 94.9 us -> 77.9 us (0.82)
  Pallas kernels: 85.8 us -> 77 us
  local copies, waits for them, and re-layouts: 8.76 us -> 0.71 us
    pallas_call x1, Pallas kernels: 85.8 us -> 77 us  [local(): pl.pallas_call(kernel, out_shape=pltpu.VMEM((M, R), BF16), in_specs=[hbm]...]
    unnamed x15 -> x1, local copies, waits for them, and re-layouts: 8.76 us -> 0.71 us
where the time goes in v2:
time: 77.9 us; the launch traced here: 77.8 us
  Pallas kernels  77 us (99%)
    pallas_call x1, Pallas kernels, local(): pl.pallas_call(kernel, out_shape=pltpu.VMEM((M, R), BF16), in_specs=[hbm]...  77 us

profile of v2, /device:TPU:1, one launch (start us, length us, event | category | flops | bytes accessed | tf_op | source)
XLA Modules:
  0.0 77.8 jit_solution(16190252919819408099)
XLA Ops:
  0.0 77.0 %feti.1 = bf16[1024,128]{1,0:T(8,128)(2,1)S(1)} custom-call(bf16[1,1,1024,128]{3,2,1,0:T(8,128)(2,1)} %slip_h.1, bf16[1,1,1024,1024]{3,2,1,0:T(8,128)(2,1)} %flex_h.1, bf16[1,1,1024,1024]{3,2,1,0:T(8,128)(2,1)} %schur_h.1, f32[12,1,1024]{2,1,0:T(1,128)} %bitcast.5, f32[192,384]{1,0:T(8,128)} %bitcast.4, f32[16]{0:T(128)} %table_h.1, s32[1,1,1024]{2,1,0:T(1,128)} %bidx_h.1, ...), custom_call_target="tpu_custom_call" | custom-call | tf_op jit(solution)/shard_map/feti/pallas_call | solution.py:366
  77.0 0.7 copy.10
